TPU v7x, 256 devices: a whole 4x4x8 slice. The times are simulated.
256 devices in a mesh: ctx: 64 (over z, y, x_hi), head: 4 (over x_lo, core).
Axes of the slice: x: 4 (x_hi: 2, x_lo: 2; x = x_hi * 2 + x_lo), y: 4, z: 8, core: 2. Of those that a mesh axis runs over, the one named last changes fastest.
Arguments:
- queries: bfloat16 [16384, 4096], P('ctx', 'head'), may hold values from -6 to 6
- keys: bfloat16 [16384, 512], P('ctx', 'head'), may hold values from -6 to 6
- values: bfloat16 [16384, 512], P('ctx', 'head'), may hold values from -24 to 24
- w_in: bfloat16 [4096, 16384], P('head', 'ctx'), may hold values from -0.09375 to 0.09375
- w_out: bfloat16 [16384, 2], P('ctx'), may hold values from -0.09375 to 0.09375
- step_pos: int32 [256], replicated, may hold values from 0 to 16383, as said below
- step_attr: int32 [256], replicated, may hold values from 0 to 3
Outputs:
- attn_out: bfloat16 [16384, 4096], P('ctx', 'head')
- step_logits: float32 [256, 2], replicated
Inputs may be any that keep to these rules, and one draw needn't show every extreme that they name: `step_pos`: strictly increasing; the last token, 16383, ends the final step. The 256 tokens of any one index of ctx hold at most 8 step ends, and some index holds exactly 8.
All inputs are finite; a program needn't handle non-finite values.
Results may differ from a plain program's by a relative error of at most 0.02.
Values may be sent and summed in bfloat16 or wider, within the bound.
A program may use at most 64 MiB of HBM per device.

v0:
```python
import math

import jax
import jax.numpy as jnp
from jax import lax
from jax.sharding import PartitionSpec as P

QH = 32
KH = 4
HD = 128
HID = 4096
CAP = 8
FEAT = 4096


negative_fill = -1e30
norm_eps = 1e-06


def block_update(state, grouped, query_pos, key_rows, value_rows, key_start):
    run_max, run_total, accum = state
    rows = key_rows.shape[0]
    kv_heads = grouped.shape[1]
    depth = grouped.shape[3]
    keys_three = key_rows.reshape(rows, kv_heads, depth)
    values_three = value_rows.reshape(rows, kv_heads, depth)
    key_pos = key_start + jnp.arange(rows, dtype=jnp.int32)
    scores = jnp.einsum(
        "qhgd,khd->hgqk", grouped, keys_three, preferred_element_type=jnp.float32
    ) * depth ** (-0.5)
    visible = (key_pos[None, None, None, :] <= query_pos[None, None, :, None]) & (
        key_pos[None, None, None, :] >= 0
    )
    block_top = jnp.max(jnp.where(visible, scores, negative_fill), axis=-1)
    new_max = jnp.maximum(run_max, block_top)
    weights = jnp.where(visible, jnp.exp(scores - new_max[..., None]), 0.0)
    fade = jnp.exp(run_max - new_max)
    run_total = run_total * fade + jnp.sum(weights, axis=-1)
    update = jnp.einsum(
        "hgqk,khd->qhgd",
        weights.astype(jnp.bfloat16),
        values_three,
        preferred_element_type=jnp.float32,
    )
    accum = accum * jnp.transpose(fade, (2, 0, 1))[..., None] + update
    return (new_max, run_total, accum)


def fold_rows(state, grouped, query_pos, key_rows, value_rows):
    rows = key_rows.shape[0]
    block = math.gcd(rows, 1024)
    last_query = jnp.max(query_pos)

    def turn(index, carry):
        begin = index * block
        key_part = lax.dynamic_slice_in_dim(key_rows, index * block, block, 0)
        value_part = lax.dynamic_slice_in_dim(value_rows, index * block, block, 0)
        needed = (begin <= last_query) & (begin + block > 0)
        return lax.cond(
            needed,
            lambda inner: block_update(inner, grouped, query_pos, key_part, value_part, begin),
            lambda inner: inner,
            carry,
        )

    return lax.fori_loop(0, rows // block, turn, state)


def start_state(count, kv_heads, group):
    run_max = jnp.full((kv_heads, group, count), negative_fill, jnp.float32)
    run_total = jnp.zeros((kv_heads, group, count), jnp.float32)
    accum = jnp.zeros((count, kv_heads, group, HD), jnp.float32)
    return (run_max, run_total, accum)


def finish_state(state):
    run_max, run_total, accum = state
    mixed = accum / jnp.transpose(run_total, (2, 0, 1))[..., None]
    return mixed.reshape(mixed.shape[0], -1).astype(jnp.bfloat16)


def make_absorb(grouped, query_pos, carry, piece):
    return fold_rows(carry, grouped, query_pos, piece[0], piece[1])


def body(queries, keys, values, w_in, w_out, step_pos, step_attr):
    ctx_rank = lax.axis_index("ctx")
    tok_rows = queries.shape[0]
    kv_heads = keys.shape[1] // HD
    group = QH // KH
    local_pos = ctx_rank * tok_rows + jnp.arange(tok_rows, dtype=jnp.int32)
    initial = start_state(tok_rows, kv_heads, group)
    grouped = queries.reshape(tok_rows, kv_heads, group, HD)
    state = make_absorb(
        grouped,
        local_pos,
        initial,
        (
            lax.all_gather(keys, "ctx", axis=0, tiled=True),
            lax.all_gather(values, "ctx", axis=0, tiled=True),
        ),
    )
    attended = finish_state(state)
    step_count = step_pos.shape[0]
    step_index = jnp.arange(step_count, dtype=jnp.int32)
    owner = step_pos // tok_rows
    owner_first = jnp.sum(
        (step_pos[None, :] < (owner * tok_rows)[:, None]).astype(jnp.int32), axis=1
    )
    slot_of = owner * CAP + (step_index - owner_first)
    my_first = jnp.sum((step_pos < ctx_rank * tok_rows).astype(jnp.int32))
    my_count = jnp.sum((step_pos < (ctx_rank + 1) * tok_rows).astype(jnp.int32)) - my_first
    slot_ids = jnp.arange(CAP, dtype=jnp.int32)
    picks = step_index[None, :] == (my_first + slot_ids)[:, None]
    slot_pos = jnp.sum(jnp.where(picks, step_pos[None, :], 0), axis=1)
    local_row = slot_pos - ctx_rank * tok_rows
    row_pick = (jnp.arange(tok_rows, dtype=jnp.int32)[None, :] == local_row[:, None]) & (
        slot_ids < my_count
    )[:, None]
    own_rows = jnp.dot(
        row_pick.astype(jnp.bfloat16), attended, preferred_element_type=jnp.float32
    ).astype(jnp.bfloat16)
    gathered = lax.all_gather(own_rows, "ctx", axis=0, tiled=True)
    partial_value = jnp.dot(gathered, w_in, preferred_element_type=jnp.float32)
    squares = jnp.sum(jnp.square(gathered.astype(jnp.float32)), axis=1)
    partial_value, squares = (
        lax.psum(partial_value.astype(jnp.bfloat16), "head").astype(jnp.float32),
        lax.psum(squares.astype(jnp.bfloat16), "head").astype(jnp.float32),
    )
    slot_total = gathered.shape[0]
    slot_match = slot_of[:, None] == jnp.arange(slot_total, dtype=jnp.int32)[None, :]
    slot_attr = jnp.sum(jnp.where(slot_match, step_attr[:, None], 0), axis=0)
    columns = w_in.shape[1]
    column_attr = (ctx_rank * columns + jnp.arange(columns, dtype=jnp.int32)) // HID
    factor = lax.rsqrt(squares / FEAT + norm_eps)
    hidden = jnp.where(
        column_attr[None, :] == slot_attr[:, None],
        jax.nn.relu(partial_value * factor[:, None]),
        0.0,
    ).astype(jnp.bfloat16)
    slot_terms = jnp.dot(hidden, w_out, preferred_element_type=jnp.float32)
    mapped = jnp.sum(jnp.where(slot_match[:, :, None], slot_terms[None, :, :], 0.0), axis=1)
    step_logits = lax.psum(mapped, "ctx")
    return (attended, step_logits)


def solution(mesh):
    in_specs = (
        P("ctx", "head"),
        P("ctx", "head"),
        P("ctx", "head"),
        P("head", "ctx"),
        P("ctx", None),
        P(),
        P(),
    )
    out_specs = (P("ctx", "head"), P())
    return jax.shard_map(body, mesh=mesh, in_specs=in_specs, out_specs=out_specs, check_vma=False)
```

profile of v0, /device:TPU:6, one launch (start us, length us, event | category | flops | bytes accessed | tf_op | source)
XLA Modules:
  0.0 735.4 jit_solution(12776863949549190865)
XLA Ops:
  7.2 0.0 copy-start
  7.2 0.0 all-gather.6.cloned.1.call-start
  7.2 1.6 copy.21
  8.8 0.0 all-gather.6.cloned.1.call-update
  8.9 0.0 all-gather.4.cloned.1.call-start
  8.9 0.7 all-gather.4.cloned.1.call-update
  9.6 0.0 all-gather.8.cloned.1.call-start
  9.7 0.6 fusion.35
  10.3 1.2 copy.20
  11.6 0.3 copy.22
  11.9 1.3 broadcast_multiply_fusion
  14.4 0.6 iota_add_fusion.2
  15.0 0.9 select_reduce_fusion.2
  15.9 120.1 %all-gather.6.cloned.1.call-done = bf16[16384,128]{0,1:T(8,128)(2,1)} async-done(((bf16[256,128]{0,1:T(8,128)(2,1)}), bf16[16384,128]{0,1:T(8,128)(2,1)}) %all-gather.6.cloned.1.call-update) | async-done | bytes 4194320 | tf_op jit(solution)/shard_map/all_gather | solution.py:100
  135.9 129.2 %all-gather.4.cloned.1.call-done = bf16[16384,128]{1,0:T(8,128)(2,1)} async-done(((bf16[256,128]{1,0:T(8,128)(2,1)}), bf16[16384,128]{1,0:T(8,128)(2,1)}) %all-gather.4.cloned.1.call-update) | async-done | bytes 4194320 | tf_op jit(solution)/shard_map/all_gather | solution.py:99
  265.1 0.1 broadcast_in_dim.106
  265.2 0.0 copy-start.1
  265.2 0.0 copy-start.2
  265.2 0.0 copy-start.3
  265.3 18.4 %while.18 = (s32[]{:T(128)}, f32[1,8,256]{2,1,0:T(8,128)S(1)}, f32[1,8,256]{2,1,0:T(8,128)S(1)}, f32[256,1,8,128]{0,3,2,1:T(8,128)S(1)}, s32[]{:T(128)}, /*index...) while((s32[]{:T(128)}, f32[1,8,256]{2,1,0:T(8,128)S(1)}, ...), condition=%wide.region_6.7_spmd.clone, body=%wide.region_1.6_spmd.clone.sunk | while | flops 1097868544 | bytes 29505884 | solution.py:66
  265.9 7.5 %conditional.3 = ((f32[1,8,256]{2,1,0:T(8,128)S(1)}, f32[1,8,256]{2,1,0:T(8,128)S(1)}, f32[256,1,8,128]{0,3,2,1:T(8,128)S(1)})) conditional(s32[]{:T(128)} %convert_element_type.88, (f32[1,8,256]{2,1,0:T(8,128)S(1)}, f32[1,8,256]{2,1,0:T(8,128)S(1)}, f32[256,1,8,128]{0,3,2,1:T(8,128)S(1)}) %tuple.61, (s32[]{:T(128)}, s32[]{:T(128)}, ...), branch_computations={%region_2.0_spmd, %region_3.5_spmd} | conditional | flops 1097868544 | bytes 29504598 | solution.py:59
  266.0 0.3 compare_and_fusion
  266.3 2.3 fusion.2
  268.7 3.0 fusion.14
  271.7 1.7 fusion.6
  283.6 0.1 divide_convert_fusion
  283.7 0.9 convolution_convert_fusion.1
  284.6 0.0 all-gather.8.cloned.1.call-update
  284.6 0.0 all-reduce.2.cloned.1.call-start
  284.7 0.0 copy-done.1
  284.7 0.2 convert_reduce_fusion
  284.9 0.0 copy-done.2
  284.9 0.1 select_reduce_fusion.1
  285.0 0.1 iota_compare_fusion
  285.2 1.0 copy.25
  286.2 221.1 %all-gather.8.cloned.1.call-done = bf16[512,1024]{1,0:T(8,128)(2,1)} async-done(((bf16[8,1024]{1,0:T(8,128)(2,1)}), bf16[512,1024]{1,0:T(8,128)(2,1)}) %all-gather.8.cloned.1.call-update) | async-done | bytes 1048592 | tf_op jit(solution)/shard_map/all_gather | solution.py:123
  507.3 0.0 copy-done
  507.3 2.4 convolution_convert_fusion
  509.7 0.0 all-reduce.2.cloned.1.call-update
  509.7 1.5 multiply_reduce_fusion
  511.2 5.7 psum.22
  516.9 31.7 %all-reduce.2.cloned.1.call-done = bf16[512,256]{1,0:T(8,128)(2,1)} async-done(((bf16[512,256]{1,0:T(8,128)(2,1)}), bf16[512,256]{1,0:T(8,128)(2,1)}) %all-reduce.2.cloned.1.call-update) | async-done | bytes 262160 | tf_op jit(solution)/shard_map/psum | solution.py:127
  548.6 0.0 copy-done.3
  548.6 1.3 fusion.28
  549.8 0.2 select_reduce_fusion
  550.1 178.9 %psum.23 = f32[256,2]{0,1:T(2,128)} all-reduce(f32[256,2]{0,1:T(2,128)S(1)} %select_reduce_fusion), channel_id=1, replica_groups=mesh['ctx'=64,'head'=4] {'ctx'}, use_global_device_ids=true, to_apply=%region_16.17 | all-reduce | flops 512 | bytes 4096 | tf_op jit(solution)/shard_map/psum | solution.py:143
  (44 shorter events, 0.3 us)
Async XLA Ops:
  7.2 500.1 %copy-start = (bf16[1024,256]{1,0:T(8,128)(2,1)S(1)}, bf16[1024,256]{1,0:T(8,128)(2,1)}, u32[]{:S(2)}) copy-start(bf16[1024,256]{1,0:T(8,128)(2,1)} %param.14) | copy-start | bytes 1572868
  7.2 128.8 %all-gather.6.cloned.1.call-start = ((), (), s32[]{:S(2)}) async-start(), calls=%async_computation.1 | async-start | bytes 4259840 | tf_op jit(solution)/shard_map/all_gather | solution.py:100
  8.9 256.2 %all-gather.4.cloned.1.call-start = ((), (), s32[]{:S(2)}) async-start(), calls=%async_computation | async-start | bytes 4259840 | tf_op jit(solution)/shard_map/all_gather | solution.py:99
  9.6 497.7 %all-gather.8.cloned.1.call-start = ((), (), s32[]{:S(2)}) async-start(), calls=%async_computation.2 | async-start | bytes 1064960 | tf_op jit(solution)/shard_map/all_gather | solution.py:123
  265.2 19.5 %copy-start.1 = (s32[256]{0:T(256)S(1)}, s32[256]{0:T(256)}, u32[]{:S(2)}) copy-start(s32[256]{0:T(256)} %param.16) | copy-start | bytes 3076
  265.2 19.7 %copy-start.2 = (s32[256]{0:T(256)S(1)}, s32[256]{0:T(256)}, u32[]{:S(2)}) copy-start(s32[256]{0:T(256)} %param.17) | copy-start | bytes 3076
  265.2 283.3 %copy-start.3 = (bf16[256,2]{0,1:T(2,128)(2,1)S(1)}, bf16[256,2]{0,1:T(2,128)(2,1)}, u32[]{:S(2)}) copy-start(bf16[256,2]{0,1:T(2,128)(2,1)} %param.15) | copy-start | bytes 3076
  284.6 263.9 %all-reduce.2.cloned.1.call-start = ((), (), s32[]{:S(2)}) async-start(), calls=%async_computation.3 | async-start | bytes 524288 | tf_op jit(solution)/shard_map/psum | solution.py:127
Sparse Core Ops, SparseCore 0:
  12.0 123.8 all-gather.5
  139.7 125.3 all-gather.3
  284.7 222.5 all-gather.7
  509.8 38.6 all-reduce.1
where the time goes:
time: 742 us; the launch traced here: 735 us
  waiting for transfers between devices  503 us (68%)
  blocking collectives  185 us (25%)
  between operations  15.1 us (2%)
  loops' own time  10.9 us (1%)
  matrix products  9.86 us (1%)
  other arithmetic  7.84 us (1%)
    all_gather x1, waiting for transfers between devices, body(): gathered = lax.all_gather(own_rows, 'ctx', axis=0, tiled=True)  221 us
    psum x1, blocking collectives, body(): step_logits = lax.psum(mapped, 'ctx')  179 us
    all_gather x1, waiting for transfers between devices, body(): lax.all_gather(keys, 'ctx', axis=0, tiled=True)  129 us
    all_gather x1, waiting for transfers between devices, body(): lax.all_gather(values, 'ctx', axis=0, tiled=True)  120 us
    psum x1, waiting for transfers between devices, body(): lax.psum(partial_value.astype(jnp.bfloat16), 'head').astype(jnp.float32)  31.7 us
  transfers between devices with their start and end apart: 4, of which 4 were waited for; matrix products, arithmetic and copies ran while one was open for 1% of the time, Pallas kernels for 0%

commit v1 on v0

v1 whole, which is shorter than its diff:
```python
import functools
import math

import jax
import jax.numpy as jnp
from jax import lax
from jax.experimental import pallas as pl
from jax.experimental.pallas import tpu as pltpu
from jax.sharding import PartitionSpec as P

HD = 128
GROUP = 8
ROWS = 256
HID = 4096
CAP = 8
FEAT = 4096
NORM_EPS = 1e-06
SCALE = HD ** -0.5 * math.log2(math.e)
HIDE = -1e30
MESH = pl.DeviceIdType.MESH
F32 = jnp.float32
BF16 = jnp.bfloat16

CHUNKS = (
    ((0, 0), (1, 0), (-1, 0), (0, 1)),
    ((0, -1), (2, 0), (-2, 0), (1, 1)),
    ((1, -1), (-1, 1), (-1, -1), (3, 0)),
    ((-3, 0), (2, 1), (2, -1), (-2, 1)),
    ((-2, -1), (4, 0), (3, 1), (3, -1)),
    ((-3, 1), (-3, -1), (4, 1), (4, -1)),
    ((0, 2), (1, 2), (-1, 2), (2, 2)),
    ((-2, 2), (3, 2), (-3, 2), (4, 2)),
)
PLACE = {spot: (n, j) for n, chunk in enumerate(CHUNKS) for j, spot in enumerate(chunk)}
DZ_ORDER = (0, 1, -1, 2, -2, 3, -3, 4)
TILES = GROUP
NCHUNK = len(CHUNKS)


def coords():
    ctx = lax.axis_index("ctx")
    head = lax.axis_index("head")
    return ctx // 8, (ctx // 2) % 4, ctx % 2, head // 2, head % 2


def device(z, y, x_hi, x_lo, core):
    return ((z * 4 + y) * 2 + x_hi, x_lo * 2 + core)


def attention_kernel(
    q_ref, k_ref, v_ref, o_ref,
    stage, kv, q_raw, q_t, acc, top, scores, tops, o_role, bias,
    swap_s, swap_r, z_s, z_r, y_s, y_r, sib_s, sib_r,
):
    z, y, x_hi, x_lo, core = coords()
    stays = x_hi == core
    swap_dev = device(z, y, core, x_lo, x_hi)
    sib_dev = device(z, y, x_hi, x_lo, 1 - core)
    z_dev = {1: device((z + 1) % 8, y, x_hi, x_lo, core), -1: device((z + 7) % 8, y, x_hi, x_lo, core)}
    y_dev = {1: device(z, (y + 1) % 4, x_hi, x_lo, core), -1: device(z, (y + 3) % 4, x_hi, x_lo, core)}

    barrier = pltpu.get_barrier_semaphore()
    for other in (sib_dev, z_dev[1], z_dev[-1], y_dev[1], y_dev[-1]):
        pl.semaphore_signal(barrier, inc=1, device_id=other, device_id_type=MESH)

    @pl.when(jnp.logical_not(stays))
    def _():
        pl.semaphore_signal(barrier, inc=1, device_id=swap_dev, device_id_type=MESH)

    stage[0:256, :] = k_ref[...]
    v32 = v_ref[...].astype(F32)
    stage[256:384, :] = v32[0:128, :].T.astype(BF16)
    stage[384:512, :] = v32[128:256, :].T.astype(BF16)

    role = (z * 4 + y) * 2 + core
    for n, chunk in enumerate(CHUNKS):
        for j, (dz, dy) in enumerate(chunk):
            for own in range(2):
                from_core = core if own == 0 else 1 - core
                origin = (((z + 8 - dz) % 8) * 4 + (y + 4 - dy) % 4) * 2 + from_core
                bias[n * 8 + own * 4 + j] = jnp.where(origin < role, 0.0, HIDE).astype(F32)

    @pl.when(stays)
    def _():
        pl.semaphore_wait(barrier, 5)

    @pl.when(jnp.logical_not(stays))
    def _():
        pl.semaphore_wait(barrier, 6)

    def spot_ref(dz, dy):
        n, j = PLACE[(dz, dy)]
        return kv.at[n, 0, j]

    def remote(src, dst, send, recv, target):
        return pltpu.make_async_remote_copy(
            src_ref=src, dst_ref=dst, send_sem=send, recv_sem=recv,
            device_id=target, device_id_type=MESH,
        )

    def swap(index, src, dst):
        return remote(src, dst, swap_s.at[index], swap_r.at[index], swap_dev)

    def local(index, src, dst):
        return pltpu.make_async_copy(src, dst, swap_r.at[index])

    def start_swap(index, src, dst):
        @pl.when(stays)
        def _():
            local(index, src, dst).start()

        @pl.when(jnp.logical_not(stays))
        def _():
            swap(index, src, dst).start()

    def wait_swap(index, src, dst):
        @pl.when(stays)
        def _():
            local(index, src, dst).wait()

        @pl.when(jnp.logical_not(stays))
        def _():
            swap(index, src, dst).wait()

    start_swap(0, stage, spot_ref(0, 0))
    start_swap(1, q_ref, q_raw)

    Z_INDEX = {1: 0, -1: 1, 2: 2, -2: 3, 3: 4, -3: 5}

    def z_copy(dz, half=None):
        step = 1 if (dz > 0 and half != 1) else -1
        if dz == 4:
            source = spot_ref(3 if half == 0 else -3, 0).at[pl.ds(half * 256, 256)]
            target = spot_ref(4, 0).at[pl.ds(half * 256, 256)]
            at = 6 + half
        else:
            source = spot_ref(dz - step, 0)
            target = spot_ref(dz, 0)
            at = Z_INDEX[dz]
        return remote(source, target, z_s.at[at], z_r.at[at], z_dev[step])

    def y_copy(dz, dy, half=None):
        base = DZ_ORDER.index(dz) * 4
        if dy == 2:
            step = 1 if half == 0 else -1
            source = spot_ref(dz, step).at[pl.ds(half * 256, 256)]
            target = spot_ref(dz, 2).at[pl.ds(half * 256, 256)]
            at = base + 2 + half
        else:
            step = dy
            source = spot_ref(dz, 0)
            target = spot_ref(dz, dy)
            at = base + (0 if dy == 1 else 1)
        return remote(source, target, y_s.at[at], y_r.at[at], y_dev[step])

    def sib_copy(n):
        return remote(kv.at[n, 0], kv.at[n, 1], sib_s.at[n], sib_r.at[n], sib_dev)

    def arrived(dz, dy):
        if (dz, dy) == (0, 0):
            pass
        elif dy == 0 and dz == 4:
            z_copy(4, 0).wait_recv()
            z_copy(4, 1).wait_recv()
        elif dy == 0:
            z_copy(dz).wait_recv()
        elif dy == 2:
            y_copy(dz, 2, 0).wait_recv()
            y_copy(dz, 2, 1).wait_recv()
        else:
            y_copy(dz, dy).wait_recv()
        if dy == 0:
            if dz == 0:
                z_copy(1).start()
                z_copy(-1).start()
            elif abs(dz) < 3:
                z_copy(dz + (1 if dz > 0 else -1)).start()
            elif dz == 3:
                z_copy(4, 0).start()
            elif dz == -3:
                z_copy(4, 1).start()
            y_copy(dz, 1).start()
            y_copy(dz, -1).start()
        elif dy == 1:
            y_copy(dz, 2, 0).start()
        elif dy == -1:
            y_copy(dz, 2, 1).start()

    def gather_chunk(n):
        for dz, dy in CHUNKS[n]:
            if (dz, dy) != (0, 0):
                arrived(dz, dy)
        sib_copy(n).start()

    wait_swap(0, stage, spot_ref(0, 0))
    arrived(0, 0)

    wait_swap(1, q_ref, q_raw)

    def flip(t, carry):
        at = pl.multiple_of(t * HD, HD)
        q_t[t] = q_raw[:, pl.ds(at, HD)].astype(F32).T.astype(BF16)
        return carry

    lax.fori_loop(0, TILES, flip, 0, unroll=True)

    ones = jnp.ones((16, 256), BF16)
    own_k = kv.at[0, 0, 0]

    def diagonal(t, carry):
        s = jnp.dot(own_k[0:256, :], q_t[t], preferred_element_type=F32)
        key = lax.broadcasted_iota(jnp.int32, (256, 256), 0)
        query = lax.broadcasted_iota(jnp.int32, (256, 256), 1)
        s = jnp.where(key <= query, s * SCALE, HIDE)
        best = jnp.max(s, axis=0, keepdims=True)
        p = jnp.exp2(s - best).astype(BF16)
        left = jnp.concatenate([own_k[256:384, :], own_k[384:512, :]], axis=1)
        left = jnp.concatenate([left, ones], axis=0)
        acc[t] = jnp.dot(left, p, preferred_element_type=F32)
        top[t] = jnp.broadcast_to(best, (8, 256))
        return carry

    lax.fori_loop(0, TILES, diagonal, 0, unroll=2)

    gather_chunk(0)
    sib_copy(0).wait_recv()

    def score(n, t, slot):
        k_all = kv[n, :, :, 0:256, :].reshape(2048, HD)
        s = jnp.dot(k_all, q_t[t], preferred_element_type=F32)
        scores[slot] = s
        best = None
        for block in range(8):
            part = jnp.max(s[block * 256:(block + 1) * 256].reshape(32, 8, 256), axis=0) + bias[n * 8 + block]
            best = part if best is None else jnp.maximum(best, part)
        tops[slot] = best

    def absorb(n, t, slot):
        old = top[t]
        new = jnp.maximum(old, jnp.max(tops[slot], axis=0, keepdims=True) * SCALE)
        top[t] = new
        fade = jnp.exp2(old - new)[:1]
        row = new[:1]
        pieces = []
        left = []
        for block in range(8):
            shift = row - bias[n * 8 + block]
            s = scores[slot, block * 256:(block + 1) * 256, :]
            pieces.append(jnp.exp2(s * SCALE - shift).astype(BF16))
            left.append(kv[n, block // 4, block % 4, 256:384, :])
            left.append(kv[n, block // 4, block % 4, 384:512, :])
        left = jnp.concatenate(left, axis=1)
        left = jnp.concatenate([left, jnp.ones((16, 2048), BF16)], axis=0)
        update = jnp.dot(left, jnp.concatenate(pieces, axis=0), preferred_element_type=F32)
        acc[t] = acc[t] * fade + update

    score(0, 0, 0)

    def pair(step, carry):
        n = step // 4
        part = step % 4
        t = part * 2
        for m in range(NCHUNK - 1):
            @pl.when((n == m) & (part == 2))
            def _():
                gather_chunk(m + 1)

        @pl.when((part == 3) & (n < NCHUNK - 1))
        def _():
            remote(kv.at[n + 1, 0], kv.at[n + 1, 1], sib_s.at[n + 1], sib_r.at[n + 1], sib_dev).wait_recv()

        score(n, t + 1, 1)
        absorb(n, t, 0)
        follow = jnp.minimum(step + 1, NCHUNK * 4 - 1)
        score(follow // 4, (follow % 4) * 2, 0)
        absorb(n, t + 1, 1)
        return carry

    lax.fori_loop(0, NCHUNK * 4, pair, 0)

    def finish(t, carry):
        at = pl.multiple_of(t * HD, HD)
        total = acc[t]
        mixed = total[0:128, :] / total[128:129, :]
        o_role[:, pl.ds(at, HD)] = mixed.T.astype(BF16)
        return carry

    lax.fori_loop(0, TILES, finish, 0, unroll=2)
    start_swap(2, o_role, o_ref)

    for dz in DZ_ORDER:
        if dz == 4:
            z_copy(4, 0).wait_send()
            z_copy(4, 1).wait_send()
        elif dz != 0:
            z_copy(dz).wait_send()
        y_copy(dz, 1).wait_send()
        y_copy(dz, -1).wait_send()
        y_copy(dz, 2, 0).wait_send()
        y_copy(dz, 2, 1).wait_send()
    for n in range(NCHUNK):
        sib_copy(n).wait_send()
    wait_swap(2, o_role, o_ref)


def attention(queries, keys, values):
    dma = pltpu.SemaphoreType.DMA
    return pl.pallas_call(
        attention_kernel,
        out_shape=jax.ShapeDtypeStruct(queries.shape, BF16),
        in_specs=[pl.BlockSpec(memory_space=pltpu.VMEM)] * 3,
        out_specs=pl.BlockSpec(memory_space=pltpu.VMEM),
        scratch_shapes=[
            pltpu.VMEM((512, HD), BF16),
            pltpu.VMEM((NCHUNK, 2, 4, 512, HD), BF16),
            pltpu.VMEM((ROWS, GROUP * HD), BF16),
            pltpu.VMEM((TILES, HD, 256), BF16),
            pltpu.VMEM((TILES, 144, 256), F32),
            pltpu.VMEM((TILES, 8, 256), F32),
            pltpu.VMEM((2, 2048, 256), F32),
            pltpu.VMEM((2, 8, 256), F32),
            pltpu.VMEM((ROWS, GROUP * HD), BF16),
            pltpu.SMEM((64,), F32),
            dma((3,)), dma((3,)), dma((8,)), dma((8,)), dma((32,)), dma((32,)), dma((NCHUNK,)), dma((NCHUNK,)),
        ],
        compiler_params=pltpu.CompilerParams(
            collective_id=0, has_side_effects=True, vmem_limit_bytes=48 * 2**20
        ),
        name="attention",
    )(queries, keys, values)


def score_kernel(
    att_ref, w_ref, w8_ref, pos_ref, col_ref, attr_ref, out_ref,
    block, other, fa, fb, part, part16, got, square, got_sq, r1, r2, r3,
    x_s, x_r, a_s, a_r, b_s, b_r, h_s, h_r, q_s, q_r, s1, t1, s2, t2, s3, t3,
):
    z, y, x_hi, x_lo, core = coords()
    ctx = lax.axis_index("ctx")
    head = lax.axis_index("head")
    me8 = x_hi * 4 + head
    x_dev = device(z, y, 1 - x_hi, x_lo, core)

    def z_at(step):
        return device((z + step) % 8, y, x_hi, x_lo, core)

    def y_at(step):
        return device(z, (y + step) % 4, x_hi, x_lo, core)

    def chip_at(step):
        other8 = (me8 + step) % 8
        return ((z * 4 + y) * 2 + other8 // 4, other8 % 4)

    barrier = pltpu.get_barrier_semaphore()
    for step in range(1, 8):
        pl.semaphore_signal(barrier, inc=1, device_id=z_at(step), device_id_type=MESH)
        pl.semaphore_signal(barrier, inc=1, device_id=chip_at(step), device_id_type=MESH)
    for step in range(1, 4):
        pl.semaphore_signal(barrier, inc=1, device_id=y_at(step), device_id_type=MESH)

    pos = pos_ref[...]
    col = col_ref[...]
    owner = pos // ROWS
    first = jnp.sum((col < owner * ROWS).astype(jnp.int32), axis=0, keepdims=True)
    step_id = lax.broadcasted_iota(jnp.int32, (1, 256), 1)
    rank = step_id - first
    slot_row = lax.broadcasted_iota(jnp.int32, (16, 256), 0)
    mine = (owner == ctx) & (rank + x_hi * CAP == slot_row)
    token = lax.broadcasted_iota(jnp.int32, (256, 256), 1)
    place = (col - ctx * ROWS == token)
    pick = jnp.dot(mine.astype(F32).astype(BF16), place.astype(F32).astype(BF16), preferred_element_type=F32)
    rows = jnp.dot(pick.astype(BF16), att_ref[...], preferred_element_type=F32)
    block[...] = rows.astype(BF16)

    pl.semaphore_wait(barrier, 17)

    def remote(src, dst, send, recv, target):
        return pltpu.make_async_remote_copy(
            src_ref=src, dst_ref=dst, send_sem=send, recv_sem=recv,
            device_id=target, device_id_type=MESH,
        )

    swap = remote(block, other, x_s, x_r, x_dev)
    swap.start()
    swap.wait()
    both = block[...] + other[...]
    fa[0, 0] = both[:, :512]
    fb[0, 0] = both[:, 512:]

    def copy_a(index, src, dst, target):
        return remote(src, dst, a_s.at[index], a_r.at[index], target)

    def copy_b(index, src, dst, target):
        return remote(src, dst, b_s.at[index], b_r.at[index], target)

    up, down = z_at(1), z_at(7)
    right, left = y_at(1), y_at(3)
    low, high = pl.ds(0, 2), pl.ds(2, 2)
    a_y1 = copy_a(0, fa.at[0, 0], fa.at[0, 1], right)
    a_y3 = copy_a(1, fa.at[0, 0], fa.at[0, 3], left)
    a_y2 = copy_a(2, fa.at[0, 1], fa.at[0, 2], right)
    a_z1 = copy_a(3, fa.at[0], fa.at[1], up)
    a_z7 = copy_a(4, fa.at[0], fa.at[7], down)
    a_z2 = copy_a(5, fa.at[1], fa.at[2], up)
    a_z6 = copy_a(6, fa.at[7], fa.at[6], down)
    a_z3 = copy_a(7, fa.at[2], fa.at[3], up)
    a_z5 = copy_a(8, fa.at[6], fa.at[5], down)
    a_4l = copy_a(9, fa.at[3, low], fa.at[4, low], up)
    a_4h = copy_a(10, fa.at[5, high], fa.at[4, high], down)
    b_z1 = copy_b(0, fb.at[0, 0], fb.at[1, 0], up)
    b_z7 = copy_b(1, fb.at[0, 0], fb.at[7, 0], down)
    b_z2 = copy_b(2, fb.at[1, 0], fb.at[2, 0], up)
    b_z6 = copy_b(3, fb.at[7, 0], fb.at[6, 0], down)
    b_z3 = copy_b(4, fb.at[2, 0], fb.at[3, 0], up)
    b_z5 = copy_b(5, fb.at[6, 0], fb.at[5, 0], down)
    b_z4 = copy_b(6, fb.at[3, 0], fb.at[4, 0], up)
    b_y1 = copy_b(7, fb.at[:, 0], fb.at[:, 1], right)
    b_y3 = copy_b(8, fb.at[:, 0], fb.at[:, 3], left)
    b_2l = copy_b(9, fb.at[pl.ds(0, 4), 1], fb.at[pl.ds(0, 4), 2], right)
    b_2h = copy_b(10, fb.at[pl.ds(4, 4), 3], fb.at[pl.ds(4, 4), 2], left)

    for c in (a_y1, a_y3, b_z1, b_z7):
        c.start()
    a_y1.wait_recv()
    a_y2.start()
    b_z1.wait_recv()
    b_z2.start()
    b_z7.wait_recv()
    b_z6.start()
    a_y3.wait_recv()
    a_y2.wait_recv()
    a_z1.start()
    a_z7.start()
    b_z2.wait_recv()
    b_z3.start()
    b_z6.wait_recv()
    b_z5.start()
    a_z1.wait_recv()
    a_z2.start()
    a_z7.wait_recv()
    a_z6.start()
    b_z3.wait_recv()
    b_z4.start()
    b_z5.wait_recv()
    b_z4.wait_recv()
    b_y1.start()
    b_y3.start()
    a_z2.wait_recv()
    a_z3.start()
    a_z6.wait_recv()
    a_z5.start()
    b_y1.wait_recv()
    b_2l.start()
    b_y3.wait_recv()
    b_2h.start()
    a_z3.wait_recv()
    a_4l.start()
    a_z5.wait_recv()
    a_4h.start()

    r = lax.broadcasted_iota(jnp.int32, (128, 256), 0)
    dz = head * 2 + r // 64
    zz = (z + 8 - dz) % 8
    yy = (y + 4 - (r // 16) % 4) % 4
    slot = ((zz * 4 + yy) * 2 + (r // 8) % 2) * CAP + r % CAP
    match = slot == owner * CAP + rank
    match32 = match.astype(F32)
    wanted = jnp.sum(jnp.where(match, (attr_ref[...] == ctx // 16).astype(F32), 0.0), axis=1, keepdims=True)

    b_2l.wait_recv()
    b_2h.wait_recv()
    a_4l.wait_recv()
    a_4h.wait_recv()

    half_a = fa[...].reshape(512, 512)
    half_b = fb[...].reshape(512, 512)
    partial = jnp.dot(half_a, w_ref[0:512, :], preferred_element_type=F32)
    partial = partial + jnp.dot(half_b, w_ref[512:1024, :], preferred_element_type=F32)
    part[...] = partial
    part16[...] = partial.astype(BF16)
    for j in range(4):
        both = jnp.zeros((128, 128), F32)
        for half in (fa, fb):
            rows32 = half[2 * j:2 * j + 2].reshape(128, 512).astype(F32)
            sq = rows32 * rows32
            for c in range(4):
                both = both + sq[:, c * 128:(c + 1) * 128]
        total = jnp.broadcast_to(jnp.sum(both, axis=1, keepdims=True), (128, 128))
        square[j] = total.T[0:8, :]

    def head_dev(step):
        return (ctx, (head + step) % 4)

    sends = []
    for step in range(1, 4):
        to = (head + step) % 4
        at = pl.ds(pl.multiple_of(to * 128, 128), 128)
        sends.append(remote(square.at[to], got_sq.at[step], q_s.at[step], q_r.at[step], head_dev(step)))
        sends.append(remote(part16.at[at], got.at[step], h_s.at[step], h_r.at[step], head_dev(step)))
    for c in sends:
        c.start()
    pre = part[pl.ds(pl.multiple_of(head * 128, 128), 128), :]
    squares = square[head]
    for c in sends:
        c.wait()
    for step in range(1, 4):
        pre = pre + got[step].astype(F32)
        squares = squares + got_sq[step]
    factor = lax.rsqrt(squares[0:1, :] / FEAT + NORM_EPS)
    factor = jnp.broadcast_to(factor, (128, 128)).T[:, 0:1]
    hidden = jnp.where(wanted > 0.5, jnp.maximum(pre * factor, 0.0), 0.0).astype(BF16)
    terms = lax.dot_general(w8_ref[...], hidden, (((1,), (1,)), ((), ())), preferred_element_type=F32)[0:8, :]
    mapped = jnp.dot(terms, match32, preferred_element_type=F32, precision=lax.Precision.HIGHEST)
    line = lax.broadcasted_iota(jnp.int32, (8, 128), 0)
    tile = jnp.where(line < 2, mapped[:, :128], mapped[:, 128:])

    def all_sum(value, buf, send, recv, me, count, at):
        buf[me] = value
        copies = []
        for step in range(1, count):
            copies.append(remote(buf.at[me], buf.at[me], send.at[step], recv.at[step], at(step)))
        for c in copies:
            c.start()
        for c in copies:
            c.wait_recv()
        total = buf[0]
        for i in range(1, count):
            total = total + buf[i]
        return total, copies

    tile, c1 = all_sum(tile, r1, s1, t1, me8, 8, chip_at)
    tile, c2 = all_sum(tile, r2, s2, t2, y, 4, y_at)
    tile, c3 = all_sum(tile, r3, s3, t3, z, 8, z_at)
    out_ref[...] = tile

    for c in c1 + c2 + c3:
        c.wait_send()
    for c in (a_y1, a_y3, a_y2, a_z1, a_z7, a_z2, a_z6, a_z3, a_z5, a_4l, a_4h):
        c.wait_send()
    for c in (b_z1, b_z7, b_z2, b_z6, b_z3, b_z5, b_z4, b_y1, b_y3, b_2l, b_2h):
        c.wait_send()


def step_scores(attended, w_in, w_out, step_pos, step_attr):
    dma = pltpu.SemaphoreType.DMA
    rows = jnp.concatenate([w_out.T, w_out.T], axis=0)
    w8 = jnp.concatenate([rows, jnp.zeros((12, 256), BF16)], axis=0)
    tile = pl.pallas_call(
        score_kernel,
        out_shape=jax.ShapeDtypeStruct((8, 128), F32),
        in_specs=[pl.BlockSpec(memory_space=pltpu.VMEM)] * 6,
        out_specs=pl.BlockSpec(memory_space=pltpu.VMEM),
        scratch_shapes=[
            pltpu.VMEM((16, 1024), BF16),
            pltpu.VMEM((16, 1024), BF16),
            pltpu.VMEM((8, 4, 16, 512), BF16),
            pltpu.VMEM((8, 4, 16, 512), BF16),
            pltpu.VMEM((512, 256), F32),
            pltpu.VMEM((512, 256), BF16),
            pltpu.VMEM((4, 128, 256), BF16),
            pltpu.VMEM((4, 8, 128), F32),
            pltpu.VMEM((4, 8, 128), F32),
            pltpu.VMEM((8, 8, 128), F32),
            pltpu.VMEM((4, 8, 128), F32),
            pltpu.VMEM((8, 8, 128), F32),
            dma, dma, dma((11,)), dma((11,)), dma((11,)), dma((11,)),
            dma((4,)), dma((4,)), dma((4,)), dma((4,)),
            dma((8,)), dma((8,)), dma((4,)), dma((4,)), dma((8,)), dma((8,)),
        ],
        compiler_params=pltpu.CompilerParams(
            collective_id=1, has_side_effects=True, vmem_limit_bytes=48 * 2**20
        ),
        name="step_scores",
    )(attended, w_in, w8, step_pos.reshape(1, 256), step_pos.reshape(256, 1), step_attr.reshape(1, 256))
    return jnp.concatenate([tile[0:2], tile[2:4]], axis=1).T


def body(queries, keys, values, w_in, w_out, step_pos, step_attr):
    attended = attention(queries, keys, values)
    return attended, step_scores(attended, w_in, w_out, step_pos, step_attr)


def solution(mesh):
    in_specs = (
        P("ctx", "head"),
        P("ctx", "head"),
        P("ctx", "head"),
        P("head", "ctx"),
        P("ctx", None),
        P(),
        P(),
    )
    out_specs = (P("ctx", "head"), P())
    return jax.shard_map(body, mesh=mesh, in_specs=in_specs, out_specs=out_specs, check_vma=False)
```

time: 742 us -> 128 us (0.17)
  waiting for transfers between devices: 503 us -> 0 us
  blocking collectives: 185 us -> 0 us
  Pallas kernels: 0 us -> 123 us
  between operations: 15.1 us -> 0.7 us
  loops' own time: 10.9 us -> 0 us
  matrix products: 9.86 us -> 0 us
    all_gather x3 -> x0, waiting for transfers between devices: 470 us -> none  [the longest x1 221 us: body(): gathered = lax.all_gather(own_rows, 'ctx', axis=0, tiled=True)]
    psum x2 -> x0, blocking collectives: 185 us -> none  [the longest x1 179 us: body(): step_logits = lax.psum(mapped, 'ctx')]
    pallas_call x0 -> x2, Pallas kernels: none -> 123 us  [the longest x1 76.1 us: attention(): pl.pallas_call(attention_kernel, out_shape=jax.ShapeDtypeStruct(queries.s...]
    psum x1 -> x0, waiting for transfers between devices: 31.7 us -> none  [body(): lax.psum(partial_value.astype(jnp.bfloat16), 'head').astype(jnp.float32)]
    another operation x17 -> x0, loops' own time: 10.9 us -> none  [the longest x1 10.6 us: fold_rows(): return lax.fori_loop(0, rows // block, turn, state)]
    dot_general x5 -> x0, matrix products: 9.86 us -> none  [the longest x1 3.03 us: block_update(): jnp.einsum('hgqk,khd->qhgd', weights.astype(jnp.bfloat16), values_three,...]
  transfers between devices with their start and end apart: 4 -> 0, of which waited for: 4 -> 0; matrix products, arithmetic and copies ran while one was open for 1% -> 0% of each run, Pallas kernels for 0% -> 0%
where the time goes in v1:
time: 128 us
  Pallas kernels  123 us (96%)
  local copies, waits for them, and re-layouts  3.99 us (3%)
    pallas_call x1, Pallas kernels, attention(): pl.pallas_call(attention_kernel, out_shape=jax.ShapeDtypeStruct(queries.s...  76.1 us
    pallas_call x1, Pallas kernels, step_scores(): pl.pallas_call(score_kernel, out_shape=jax.ShapeDtypeStruct((8, 128), F32...  46.7 us
    unnamed x15, local copies, waits for them, and re-layouts  3.77 us

profile of v1, /device:TPU:6, one launch (start us, length us, event | category | flops | bytes accessed | tf_op | source)
XLA Modules:
  0.0 128.1 jit_solution(1560047813417665014)
XLA Ops:
  0.6 0.0 copy-start.6
  0.7 0.1 pad.4.clone
  0.7 0.6 copy-done.6
  1.3 0.0 copy-start.4
  1.3 0.1 maximum_maximum_fusion.w8_ref
  1.4 0.6 copy-done.4
  2.0 0.0 copy-start.2
  2.0 0.0 copy-start.3
  2.0 0.1 copy.9.col_ref
  2.1 0.7 copy-done.2
  2.8 0.0 copy-done.3
  2.9 0.0 copy-start.1
  2.9 1.0 copy-done.1
  3.9 0.0 copy-start
  3.9 0.0 copy-start.5
  3.9 76.1 %attention.1.att_ref = bf16[256,1024]{1,0:T(8,128)(2,1)S(1)} custom-call(bf16[256,1024]{1,0:T(8,128)(2,1)S(1)} %copy-done.1, bf16[256,128]{1,0:T(8,128)(2,1)S(1)} %copy-done.2, bf16[256,128]{1,0:T(8,128)(2,1)S(1)} %copy-done.3), custom_call_target="tpu_custom_call" | custom-call | tf_op jit(solution)/shard_map/attention/pallas_call | solution.py:308
  80.0 0.0 copy-done
  80.0 0.0 copy-done.5
  80.0 46.7 %step_scores.1 = f32[8,128]{1,0:T(8,128)S(1)} custom-call(bf16[256,1024]{1,0:T(8,128)(2,1)S(1)} %attention.1.att_ref, bf16[1024,256]{1,0:T(8,128)(2,1)S(1)} %copy-done, bf16[16,256]{1,0:T(8,128)(2,1)S(1)} %maximum_maximum_fusion.w8_ref, s32[1,256]{1,0:T(1,128)S(1)} %bitcast.7, s32[256,1]{1,0:T(8,128)S(1)} %copy.9.col_ref, s32[1,256]{1,0:T(1,128)S(1)} %bitcast.8), custom_call_target="tpu_custom_call" | custom-call | tf_op jit(solution)/shard_map/step_scores/pallas_call | solution.py:548
  126.7 0.6 maximum_bitcast_fusion
  127.3 0.8 copy.11
  (2 shorter events, 0.0 us)
Async XLA Ops:
  0.6 0.7 copy-start.6
  1.3 0.7 copy-start.4
  2.0 0.8 copy-start.2
  2.0 0.9 copy-start.3
  2.9 1.0 copy-start.1
  3.9 76.1 %copy-start = (bf16[1024,256]{1,0:T(8,128)(2,1)S(1)}, bf16[1024,256]{1,0:T(8,128)(2,1)}, u32[]{:S(2)}) copy-start(bf16[1024,256]{1,0:T(8,128)(2,1)} %w_ref.1) | copy-start | bytes 1572868
  3.9 76.1 %copy-start.5 = (s32[256]{0:T(256)S(1)}, s32[256]{0:T(256)}, u32[]{:S(2)}) copy-start(s32[256]{0:T(256)} %param.13) | copy-start | bytes 3076

commit v2 on v1

v2 whole, which is shorter than its diff:
```python
import functools
import math

import jax
import jax.numpy as jnp
from jax import lax
from jax.experimental import pallas as pl
from jax.experimental.pallas import tpu as pltpu
from jax.sharding import PartitionSpec as P

HD = 128
GROUP = 8
ROWS = 256
HID = 4096
CAP = 8
FEAT = 4096
NORM_EPS = 1e-06
SCALE = HD ** -0.5 * math.log2(math.e)
HIDE = -1e30
MESH = pl.DeviceIdType.MESH
F32 = jnp.float32
BF16 = jnp.bfloat16

CHUNKS = (
    ((0, 0), (1, 0), (-1, 0), (0, 1)),
    ((0, -1), (2, 0), (-2, 0), (1, 1)),
    ((1, -1), (-1, 1), (-1, -1), (3, 0)),
    ((-3, 0), (2, 1), (2, -1), (-2, 1)),
    ((-2, -1), (4, 0), (3, 1), (3, -1)),
    ((-3, 1), (-3, -1), (4, 1), (4, -1)),
    ((0, 2), (1, 2), (-1, 2), (2, 2)),
    ((-2, 2), (3, 2), (-3, 2), (4, 2)),
)
PLACE = {spot: (n, j) for n, chunk in enumerate(CHUNKS) for j, spot in enumerate(chunk)}
DZ_ORDER = (0, 1, -1, 2, -2, 3, -3, 4)
TILES = GROUP
NCHUNK = len(CHUNKS)


def coords():
    ctx = lax.axis_index("ctx")
    head = lax.axis_index("head")
    return ctx // 8, (ctx // 2) % 4, ctx % 2, head // 2, head % 2


def device(z, y, x_hi, x_lo, core):
    return ((z * 4 + y) * 2 + x_hi, x_lo * 2 + core)


EVENT = (0, 2, 5, 8, 11, 14, 17, 20)
SPLIT = (21, 28, 32)


def fused_kernel(
    q_ref, k_ref, v_ref, w_ref, w_out_ref, pos_ref, attr_ref,
    o_ref, logit_ref,
    stage, v_in, kv, q_raw, q_t, acc, top, scores, tops, o_role, bias,
    qs_t, s_scores, s_acc, s_top, w_v,
    block, other, fa, fb, own_a, own_b, part, part16, got, square, got_sq, r1, r2, r3,
    load, swap_s, swap_r, z_s, z_r, y_s, y_r, sib_s, sib_r,
    x_s, x_r, a_s, a_r, b_s, b_r, h_s, h_r, g_s, g_r, s1, t1, s2, t2, s3, t3,
):
    z, y, x_hi, x_lo, core = coords()
    ctx = lax.axis_index("ctx")
    head = lax.axis_index("head")
    me8 = x_hi * 4 + head
    stays = x_hi == core
    sib_dev = device(z, y, x_hi, x_lo, 1 - core)

    def z_at(step):
        return device((z + step) % 8, y, x_hi, x_lo, core)

    def y_at(step):
        return device(z, (y + step) % 4, x_hi, x_lo, core)

    def chip_at(step):
        other8 = (me8 + step) % 8
        return ((z * 4 + y) * 2 + other8 // 4, other8 % 4)

    def flip_at(z_step, y_step):
        return device((z + z_step) % 8, (y + y_step) % 4, core, x_lo, x_hi)

    swap_dev = flip_at(0, 0)
    z_dev = {1: z_at(1), -1: z_at(7)}
    y_dev = {1: y_at(1), -1: y_at(3)}

    barrier = pltpu.get_barrier_semaphore()

    def greet(target):
        pl.semaphore_signal(barrier, inc=1, device_id=target, device_id_type=MESH)

    for step in range(1, 8):
        greet(z_at(step))
        greet(flip_at(step, 0))
        greet(chip_at(step))
    for step in range(1, 4):
        greet(y_at(step))
        greet(flip_at(0, step))

    get_k = pltpu.make_async_copy(k_ref, stage.at[pl.ds(0, 256)], load.at[0])
    get_v = pltpu.make_async_copy(v_ref, v_in, load.at[1])
    get_w = pltpu.make_async_copy(w_ref, w_v, load.at[2])
    get_v.start()
    get_k.start()
    get_w.start()

    role = (z * 4 + y) * 2 + core
    for n, chunk in enumerate(CHUNKS):
        for j, (dz, dy) in enumerate(chunk):
            for own in range(2):
                from_core = core if own == 0 else 1 - core
                origin = (((z + 8 - dz) % 8) * 4 + (y + 4 - dy) % 4) * 2 + from_core
                bias[n * 8 + own * 4 + j] = jnp.where(origin < role, 0.0, HIDE).astype(F32)

    get_v.wait()
    v32 = v_in[...].astype(F32)
    stage[256:384, :] = v32[0:128, :].T.astype(BF16)
    stage[384:512, :] = v32[128:256, :].T.astype(BF16)
    get_k.wait()

    pl.semaphore_wait(barrier, 27)

    def spot_ref(dz, dy):
        n, j = PLACE[(dz, dy)]
        return kv.at[n, 0, j]

    def remote(src, dst, send, recv, target):
        return pltpu.make_async_remote_copy(
            src_ref=src, dst_ref=dst, send_sem=send, recv_sem=recv,
            device_id=target, device_id_type=MESH,
        )

    def start_flip(src, dst, send, recv):
        @pl.when(stays)
        def _():
            pltpu.make_async_copy(src, dst, recv).start()

        @pl.when(jnp.logical_not(stays))
        def _():
            remote(src, dst, send, recv, swap_dev).start()

    def wait_flip(src, dst, send, recv):
        @pl.when(stays)
        def _():
            pltpu.make_async_copy(src, dst, recv).wait()

        @pl.when(jnp.logical_not(stays))
        def _():
            remote(src, dst, send, recv, swap_dev).wait()

    kv_flip = (stage, spot_ref(0, 0), swap_s.at[0], swap_r.at[0])
    q_flip = (q_ref, q_raw, swap_s.at[1], swap_r.at[1])
    o_flip = (o_role, o_ref, swap_s.at[2], swap_r.at[2])
    start_flip(*kv_flip)
    start_flip(*q_flip)

    Z_INDEX = {1: 0, -1: 1, 2: 2, -2: 3, 3: 4, -3: 5}

    def z_copy(dz, half=None):
        step = 1 if (dz > 0 and half != 1) else -1
        if dz == 4:
            source = spot_ref(3 if half == 0 else -3, 0).at[pl.ds(half * 256, 256)]
            target = spot_ref(4, 0).at[pl.ds(half * 256, 256)]
            at = 6 + half
        else:
            source = spot_ref(dz - step, 0)
            target = spot_ref(dz, 0)
            at = Z_INDEX[dz]
        return remote(source, target, z_s.at[at], z_r.at[at], z_dev[step])

    def y_copy(dz, dy, half=None):
        base = DZ_ORDER.index(dz) * 4
        if dy == 2:
            step = 1 if half == 0 else -1
            source = spot_ref(dz, step).at[pl.ds(half * 256, 256)]
            target = spot_ref(dz, 2).at[pl.ds(half * 256, 256)]
            at = base + 2 + half
        else:
            step = dy
            source = spot_ref(dz, 0)
            target = spot_ref(dz, dy)
            at = base + (0 if dy == 1 else 1)
        return remote(source, target, y_s.at[at], y_r.at[at], y_dev[step])

    def sib_copy(n):
        return remote(kv.at[n, 0], kv.at[n, 1], sib_s.at[n], sib_r.at[n], sib_dev)

    def arrived(dz, dy):
        if (dz, dy) == (0, 0):
            pass
        elif dy == 0 and dz == 4:
            z_copy(4, 0).wait_recv()
            z_copy(4, 1).wait_recv()
        elif dy == 0:
            z_copy(dz).wait_recv()
        elif dy == 2:
            y_copy(dz, 2, 0).wait_recv()
            y_copy(dz, 2, 1).wait_recv()
        else:
            y_copy(dz, dy).wait_recv()
        if dy == 0:
            if dz == 0:
                z_copy(1).start()
                z_copy(-1).start()
            elif abs(dz) < 3:
                z_copy(dz + (1 if dz > 0 else -1)).start()
            elif dz == 3:
                z_copy(4, 0).start()
            elif dz == -3:
                z_copy(4, 1).start()
            y_copy(dz, 1).start()
            y_copy(dz, -1).start()
        elif dy == 1:
            y_copy(dz, 2, 0).start()
        elif dy == -1:
            y_copy(dz, 2, 1).start()

    def gather_chunk(n):
        for dz, dy in CHUNKS[n]:
            if (dz, dy) != (0, 0):
                arrived(dz, dy)
        sib_copy(n).start()

    pos = pos_ref[...]
    col = jnp.broadcast_to(pos.astype(F32), (128, 256)).T[:, 0:1].astype(jnp.int32)
    owner = pos // ROWS
    first = jnp.sum((col < owner * ROWS).astype(jnp.int32), axis=0, keepdims=True)
    rank = lax.broadcasted_iota(jnp.int32, (1, 256), 1) - first
    owner_col = col // ROWS
    first_col = jnp.sum((pos < owner_col * ROWS).astype(jnp.int32), axis=1, keepdims=True)
    rank_col = lax.broadcasted_iota(jnp.int32, (256, 1), 0) - first_col
    lane = lax.broadcasted_iota(jnp.int32, (256, 128), 1)
    held = (owner_col == role) & (rank_col == lane % CAP)
    s_row = jnp.sum(jnp.where(held, col - role * ROWS, 0), axis=0, keepdims=True)
    mine = (owner == role) & (rank == lax.broadcasted_iota(jnp.int32, (16, 256), 0))
    place = col - role * ROWS == lax.broadcasted_iota(jnp.int32, (256, 256), 1)
    pick = jnp.dot(mine.astype(F32).astype(BF16), place.astype(F32).astype(BF16), preferred_element_type=F32)
    pick = pick.astype(BF16)

    wait_flip(*kv_flip)
    arrived(0, 0)
    wait_flip(*q_flip)

    def turn(t, carry):
        at = pl.multiple_of(t * HD, HD)
        q_t[t] = q_raw[:, pl.ds(at, HD)].astype(F32).T.astype(BF16)
        return carry

    lax.fori_loop(0, TILES, turn, 0, unroll=True)
    s_rows = jnp.dot(pick, q_raw[...], preferred_element_type=F32)
    stacked = [s_rows[0:8, h * HD:(h + 1) * HD] for h in range(GROUP)]
    stacked = jnp.concatenate(stacked + [jnp.zeros((64, HD), F32)], axis=0)
    qs_t[...] = stacked.T.astype(BF16)

    own_k = kv.at[0, 0, 0]

    def values_of(ref):
        return jnp.concatenate([ref[256:384, :], ref[384:512, :]], axis=1)

    def first_block(q, last):
        width = q.shape[1]
        s = jnp.dot(own_k[0:256, :], q, preferred_element_type=F32)
        key = lax.broadcasted_iota(jnp.int32, (256, width), 0)
        s = jnp.where(key <= last, s * SCALE, HIDE)
        best = jnp.max(s, axis=0, keepdims=True)
        p = jnp.exp2(s - best).astype(BF16)
        left = jnp.concatenate([values_of(own_k), jnp.ones((16, 256), BF16)], axis=0)
        return jnp.dot(left, p, preferred_element_type=F32), jnp.broadcast_to(best, (8, width))

    def diagonal(t, carry):
        query = lax.broadcasted_iota(jnp.int32, (256, 256), 1)
        acc[t], top[t] = first_block(q_t[t], query)
        return carry

    s_acc[...], s_top[...] = first_block(qs_t[...], s_row)
    lax.fori_loop(0, TILES, diagonal, 0, unroll=2)

    def keys_of(n):
        return kv[n, :, :, 0:256, :].reshape(2048, HD)

    def best_of(s, n):
        best = None
        for at in range(8):
            part_best = jnp.max(s[at * 256:(at + 1) * 256].reshape(32, 8, s.shape[1]), axis=0) + bias[n * 8 + at]
            best = part_best if best is None else jnp.maximum(best, part_best)
        return best

    def mix(n, s_of, row):
        pieces = []
        left = []
        for at in range(8):
            shift = row - bias[n * 8 + at]
            pieces.append(jnp.exp2(s_of(at) * SCALE - shift).astype(BF16))
            left.append(kv[n, at // 4, at % 4, 256:384, :])
            left.append(kv[n, at // 4, at % 4, 384:512, :])
        left = jnp.concatenate(left, axis=1)
        left = jnp.concatenate([left, jnp.ones((16, 2048), BF16)], axis=0)
        return jnp.dot(left, jnp.concatenate(pieces, axis=0), preferred_element_type=F32)

    def score(n, t, slot):
        s = jnp.dot(keys_of(n), q_t[t], preferred_element_type=F32)
        scores[slot] = s
        tops[slot] = best_of(s, n)

    def absorb(n, t, slot):
        old = top[t]
        new = jnp.maximum(old, jnp.max(tops[slot], axis=0, keepdims=True) * SCALE)
        top[t] = new
        fade = jnp.exp2(old - new)[:1]
        update = mix(n, lambda at: scores[slot, at * 256:(at + 1) * 256, :], new[:1])
        acc[t] = acc[t] * fade + update

    def step_rows(n):
        s = jnp.dot(keys_of(n), qs_t[...], preferred_element_type=F32)
        s_scores[...] = s
        old = s_top[...]
        new = jnp.maximum(old, jnp.max(best_of(s, n), axis=0, keepdims=True) * SCALE)
        s_top[...] = new
        fade = jnp.exp2(old - new)[:1]
        update = mix(n, lambda at: s_scores[at * 256:(at + 1) * 256, :], new[:1])
        s_acc[...] = s_acc[...] * fade + update

    def pair(step, carry):
        n = step // 4
        t = (step % 4) * 2
        score(n, t + 1, 1)
        absorb(n, t, 0)
        follow = jnp.minimum(step + 1, NCHUNK * 4 - 1)
        score(follow // 4, (follow % 4) * 2, 0)
        absorb(n, t + 1, 1)
        return carry

    def turn_a(step, carry):
        for m in range(1, NCHUNK):
            @pl.when(step == EVENT[m])
            def _():
                gather_chunk(m)

        due = jnp.int32(0)
        fresh = step == EVENT[1] + 1
        for m in range(1, NCHUNK):
            due = due + (step > EVENT[m]).astype(jnp.int32)
            fresh = fresh | (step == EVENT[m] + 1)

        @pl.when(fresh)
        def _():
            remote(kv.at[due, 0], kv.at[due, 1], sib_s.at[due], sib_r.at[due], sib_dev).wait_recv()
            step_rows(due)

        return pair(step, carry)

    gather_chunk(0)
    sib_copy(0).wait_recv()
    step_rows(0)
    score(0, 0, 0)
    lax.fori_loop(0, SPLIT[0], turn_a, 0)
    sib_copy(7).wait_recv()
    step_rows(7)

    done = s_acc[...]
    mixed = (done[0:128, :] / done[128:129, :]).T
    row8 = jnp.concatenate([mixed[h * 8:(h + 1) * 8, :] for h in range(GROUP)], axis=1)
    row16 = jnp.concatenate([row8, row8], axis=0)
    row_id = lax.broadcasted_iota(jnp.int32, (16, 1024), 0)
    block[...] = jnp.where(row_id // CAP == core, row16, 0.0).astype(BF16)
    pair_up = remote(block, other, x_s, x_r, sib_dev)
    pair_up.start()
    pair_up.wait()
    both = block[...] + other[...]
    own_a[...] = both[:, :512]
    own_b[...] = both[:, 512:]

    def copy_a(index, src, dst, target):
        return remote(src, dst, a_s.at[index], a_r.at[index], target)

    def copy_b(index, src, dst, target):
        return remote(src, dst, b_s.at[index], b_r.at[index], target)

    flip_b = (own_b, fb.at[0, 0], b_s.at[0], b_r.at[0])
    flip_a = (own_a, fa.at[0, 0], a_s.at[0], a_r.at[0])
    b_z = [copy_b(k, own_b, fb.at[k, 0], flip_at(k, 0)) for k in range(1, 8)]
    a_y = [copy_a(k, own_a, fa.at[0, k], flip_at(0, k)) for k in range(1, 4)]
    start_flip(*flip_a)
    start_flip(*flip_b)
    for c in a_y + b_z:
        c.start()

    lax.fori_loop(SPLIT[0], SPLIT[1], pair, 0)

    low, high = pl.ds(0, 2), pl.ds(2, 2)
    a_z = [copy_a(3 + k, fa.at[0], fa.at[d % 8], z_at(d % 8)) for k, d in ((1, 1), (2, -1), (3, 2), (4, -2))]
    a_far = [
        copy_a(8, fa.at[2], fa.at[3], z_at(1)),
        copy_a(9, fa.at[6], fa.at[5], z_at(7)),
        copy_a(10, fa.at[2, low], fa.at[4, low], z_at(2)),
        copy_a(11, fa.at[6, high], fa.at[4, high], z_at(6)),
    ]
    b_y = [copy_b(7 + k, fb.at[:, 0], fb.at[:, k], y_at(k)) for k in (1, 3, 2)]

    wait_flip(*flip_a)
    for c in a_y:
        c.wait_recv()
    for c in a_z:
        c.start()
    wait_flip(*flip_b)
    for c in b_z:
        c.wait_recv()
    for c in b_y:
        c.start()

    lax.fori_loop(SPLIT[1], SPLIT[2], pair, 0)

    def finish(t, carry):
        at = pl.multiple_of(t * HD, HD)
        total = acc[t]
        o_role[:, pl.ds(at, HD)] = (total[0:128, :] / total[128:129, :]).T.astype(BF16)
        return carry

    for c in a_z:
        c.wait_recv()
    for c in a_far:
        c.start()
    lax.fori_loop(0, TILES, finish, 0, unroll=2)
    start_flip(*o_flip)

    r = lax.broadcasted_iota(jnp.int32, (128, 256), 0)
    dz = head * 2 + r // 64
    zz = (z + 8 - dz) % 8
    yy = (y + 4 - (r // 16) % 4) % 4
    slot = ((zz * 4 + yy) * 2 + (r // 8) % 2) * CAP + r % CAP
    match = slot == owner * CAP + rank
    match32 = match.astype(F32)
    wanted = jnp.sum(jnp.where(match, (attr_ref[...] == ctx // 16).astype(F32), 0.0), axis=1, keepdims=True)

    w32 = w_out_ref[...].astype(F32)
    odd = lax.broadcasted_iota(jnp.int32, (256, 128), 1) % 2 == 1
    w16 = jnp.where(odd, w32[:, 1:2], w32[:, 0:1]).T[0:16, :].astype(BF16)
    get_w.wait()
    for c in b_y + a_far:
        c.wait_recv()

    half_a = fa[...].reshape(512, 512)
    half_b = fb[...].reshape(512, 512)
    partial = jnp.dot(half_a, w_v[0:512, :], preferred_element_type=F32)
    partial = partial + jnp.dot(half_b, w_v[512:1024, :], preferred_element_type=F32)
    part[...] = partial
    part16[...] = partial.astype(BF16)
    for j in range(4):
        summed = jnp.zeros((128, 128), F32)
        for half in (fa, fb):
            rows32 = half[2 * j:2 * j + 2].reshape(128, 512).astype(F32)
            sq = rows32 * rows32
            for c in range(4):
                summed = summed + sq[:, c * 128:(c + 1) * 128]
        total = jnp.broadcast_to(jnp.sum(summed, axis=1, keepdims=True), (128, 128))
        square[j] = total.T[0:8, :]

    def head_dev(step):
        return (ctx, (head + step) % 4)

    sends = []
    for step in range(1, 4):
        to = (head + step) % 4
        at = pl.ds(pl.multiple_of(to * 128, 128), 128)
        sends.append(remote(square.at[to], got_sq.at[step], g_s.at[step], g_r.at[step], head_dev(step)))
        sends.append(remote(part16.at[at], got.at[step], h_s.at[step], h_r.at[step], head_dev(step)))
    for c in sends:
        c.start()
    pre = part[pl.ds(pl.multiple_of(head * 128, 128), 128), :]
    squares = square[head]
    for c in sends:
        c.wait()
    for step in range(1, 4):
        pre = pre + got[step].astype(F32)
        squares = squares + got_sq[step]
    factor = lax.rsqrt(squares[0:1, :] / FEAT + NORM_EPS)
    factor = jnp.broadcast_to(factor, (128, 128)).T[:, 0:1]
    hidden = jnp.where(wanted > 0.5, jnp.maximum(pre * factor, 0.0), 0.0).astype(BF16)
    terms = lax.dot_general(w16, hidden, (((1,), (1,)), ((), ())), preferred_element_type=F32)[0:8, :]
    mapped = jnp.dot(terms, match32, preferred_element_type=F32, precision=lax.Precision.HIGHEST)
    line = lax.broadcasted_iota(jnp.int32, (8, 128), 0)
    tile = jnp.where(line < 2, mapped[:, :128], mapped[:, 128:])

    def all_sum(value, buf, send, recv, me, count, at):
        buf[me] = value
        copies = []
        for step in range(1, count):
            copies.append(remote(buf.at[me], buf.at[me], send.at[step], recv.at[step], at(step)))
        for c in copies:
            c.start()
        for c in copies:
            c.wait_recv()
        total = buf[0]
        for i in range(1, count):
            total = total + buf[i]
        return total, copies

    tile, c1 = all_sum(tile, r1, s1, t1, me8, 8, chip_at)
    tile, c2 = all_sum(tile, r2, s2, t2, y, 4, y_at)
    tile, c3 = all_sum(tile, r3, s3, t3, z, 8, z_at)
    logit_ref[...] = tile

    for c in c1 + c2 + c3 + a_y + a_z + a_far + b_z + b_y:
        c.wait_send()
    for dz in DZ_ORDER:
        if dz == 4:
            z_copy(4, 0).wait_send()
            z_copy(4, 1).wait_send()
        elif dz != 0:
            z_copy(dz).wait_send()
        y_copy(dz, 1).wait_send()
        y_copy(dz, -1).wait_send()
        y_copy(dz, 2, 0).wait_send()
        y_copy(dz, 2, 1).wait_send()
    for n in range(NCHUNK):
        sib_copy(n).wait_send()
    wait_flip(*o_flip)


def body(queries, keys, values, w_in, w_out, step_pos, step_attr):
    dma = pltpu.SemaphoreType.DMA
    vmem = pltpu.VMEM
    here = pl.BlockSpec(memory_space=pltpu.VMEM)
    away = pl.BlockSpec(memory_space=pl.ANY)
    attended, tile = pl.pallas_call(
        fused_kernel,
        out_shape=(
            jax.ShapeDtypeStruct(queries.shape, BF16),
            jax.ShapeDtypeStruct((8, 128), F32),
        ),
        in_specs=[away] * 4 + [here] * 3,
        out_specs=(here, here),
        scratch_shapes=[
            vmem((512, HD), BF16),
            vmem((ROWS, HD), BF16),
            vmem((NCHUNK, 2, 4, 512, HD), BF16),
            vmem((ROWS, GROUP * HD), BF16),
            vmem((TILES, HD, 256), BF16),
            vmem((TILES, 144, 256), F32),
            vmem((TILES, 8, 256), F32),
            vmem((2, 2048, 256), F32),
            vmem((2, 8, 256), F32),
            vmem((ROWS, GROUP * HD), BF16),
            pltpu.SMEM((64,), F32),
            vmem((HD, 128), BF16),
            vmem((2048, 128), F32),
            vmem((144, 128), F32),
            vmem((8, 128), F32),
            vmem((1024, 256), BF16),
            vmem((16, 1024), BF16),
            vmem((16, 1024), BF16),
            vmem((8, 4, 16, 512), BF16),
            vmem((8, 4, 16, 512), BF16),
            vmem((16, 512), BF16),
            vmem((16, 512), BF16),
            vmem((512, 256), F32),
            vmem((512, 256), BF16),
            vmem((4, 128, 256), BF16),
            vmem((4, 8, 128), F32),
            vmem((4, 8, 128), F32),
            vmem((8, 8, 128), F32),
            vmem((4, 8, 128), F32),
            vmem((8, 8, 128), F32),
            dma((3,)), dma((3,)), dma((3,)), dma((8,)), dma((8,)), dma((32,)), dma((32,)),
            dma((NCHUNK,)), dma((NCHUNK,)),
            dma, dma, dma((12,)), dma((12,)), dma((11,)), dma((11,)),
            dma((4,)), dma((4,)), dma((4,)), dma((4,)),
            dma((8,)), dma((8,)), dma((4,)), dma((4,)), dma((8,)), dma((8,)),
        ],
        compiler_params=pltpu.CompilerParams(
            collective_id=0, has_side_effects=True, vmem_limit_bytes=60 * 2**20
        ),
        name="trace_scores",
    )(queries, keys, values, w_in, w_out, step_pos.reshape(1, 256), step_attr.reshape(1, 256))
    return attended, jnp.concatenate([tile[0:2], tile[2:4]], axis=1).T


def solution(mesh):
    in_specs = (
        P("ctx", "head"),
        P("ctx", "head"),
        P("ctx", "head"),
        P("head", "ctx"),
        P("ctx", None),
        P(),
        P(),
    )
    out_specs = (P("ctx", "head"), P())
    return jax.shard_map(body, mesh=mesh, in_specs=in_specs, out_specs=out_specs, check_vma=False)
```

time: 128 us -> 113 us (0.88); the launches traced: 128 us -> 111 us
  Pallas kernels: 123 us -> 105 us
    pallas_call x2 -> x1, Pallas kernels: 123 us -> 105 us  [body(): pl.pallas_call(fused_kernel, out_shape=(jax.ShapeDtypeStruct(queries.shap...]
    unnamed x15 -> x2, local copies, waits for them, and re-layouts: 3.77 us -> 3.3 us
where the time goes in v2:
time: 113 us; the launch traced here: 111 us
  Pallas kernels  105 us (93%)
  local copies, waits for them, and re-layouts  4.06 us (4%)
    pallas_call x1, Pallas kernels, body(): pl.pallas_call(fused_kernel, out_shape=(jax.ShapeDtypeStruct(queries.shap...  105 us
    unnamed x2, local copies, waits for them, and re-layouts  3.3 us

profile of v2, /device:TPU:6, one launch (start us, length us, event | category | flops | bytes accessed | tf_op | source)
XLA Modules:
  0.0 110.6 jit_solution(16129228895878807542)
XLA Ops:
  0.6 1.4 %copy.9.w_out_ref = bf16[256,2]{1,0:T(8,128)(2,1)} copy(bf16[256,2]{0,1:T(2,128)(2,1)} %param.11) | data formatting | bytes 2048 | tf_op args[4]
  2.1 105.3 %trace_scores.1 = (bf16[256,1024]{1,0:T(8,128)(2,1)}, f32[8,128]{1,0:T(8,128)}) custom-call(bf16[256,1024]{1,0:T(8,128)(2,1)} %q_ref.1, bf16[256,128]{1,0:T(8,128)(2,1)} %k_ref.1, bf16[256,128]{1,0:T(8,128)(2,1)} %v_ref.1, bf16[1024,256]{1,0:T(8,128)(2,1)} %w_ref.1, bf16[256,2]{1,0:T(8,128)(2,1)} %copy.9.w_out_ref, s32[1,256]{1,0:T(1,128)} %bitcast.4, ...), custom_call_target="tpu_custom_call" | custom-call | tf_op jit(solution)/shard_map/trace_scores/pallas_call | solution.py:525
  107.4 0.8 fusion
  108.2 0.6 maximum_bitcast_fusion
  108.7 1.9 %copy.11 = bf16[256,1024]{1,0:T(8,128)(2,1)} copy(bf16[256,1024]{1,0:T(8,128)(2,1)} %get-tuple-element.10) | data formatting | bytes 1048576

commit v3 on v2

--- a/solution.py
+++ b/solution.py
@@ -47,8 +47,8 @@
     return ((z * 4 + y) * 2 + x_hi, x_lo * 2 + core)
 
 
-EVENT = (0, 2, 5, 8, 11, 14, 17, 20)
-SPLIT = (21, 28, 32)
+EVENT = (0, 0, 0, 3, 5, 8, 10, 13)
+SPLIT = (14, 18, 21, 24, 29, 32)
 
 
 def fused_kernel(
@@ -152,7 +152,6 @@
     q_flip = (q_ref, q_raw, swap_s.at[1], swap_r.at[1])
     o_flip = (o_role, o_ref, swap_s.at[2], swap_r.at[2])
     start_flip(*kv_flip)
-    start_flip(*q_flip)
 
     Z_INDEX = {1: 0, -1: 1, 2: 2, -2: 3, 3: 4, -3: 5}
 
@@ -221,6 +220,10 @@
                 arrived(dz, dy)
         sib_copy(n).start()
 
+    wait_flip(*kv_flip)
+    arrived(0, 0)
+    start_flip(*q_flip)
+
     pos = pos_ref[...]
     col = jnp.broadcast_to(pos.astype(F32), (128, 256)).T[:, 0:1].astype(jnp.int32)
     owner = pos // ROWS
@@ -237,8 +240,7 @@
     pick = jnp.dot(mine.astype(F32).astype(BF16), place.astype(F32).astype(BF16), preferred_element_type=F32)
     pick = pick.astype(BF16)
 
-    wait_flip(*kv_flip)
-    arrived(0, 0)
+    gather_chunk(0)
     wait_flip(*q_flip)
 
     def turn(t, carry):
@@ -273,6 +275,7 @@
         return carry
 
     s_acc[...], s_top[...] = first_block(qs_t[...], s_row)
+    gather_chunk(1)
     lax.fori_loop(0, TILES, diagonal, 0, unroll=2)
 
     def keys_of(n):
@@ -331,14 +334,14 @@
         return carry
 
     def turn_a(step, carry):
-        for m in range(1, NCHUNK):
+        for m in range(2, NCHUNK):
             @pl.when(step == EVENT[m])
             def _():
                 gather_chunk(m)
 
-        due = jnp.int32(0)
-        fresh = step == EVENT[1] + 1
-        for m in range(1, NCHUNK):
+        due = jnp.int32(1)
+        fresh = step == EVENT[2] + 1
+        for m in range(2, NCHUNK):
             due = due + (step > EVENT[m]).astype(jnp.int32)
             fresh = fresh | (step == EVENT[m] + 1)
 
@@ -349,9 +352,10 @@
 
         return pair(step, carry)
 
-    gather_chunk(0)
     sib_copy(0).wait_recv()
     step_rows(0)
+    sib_copy(1).wait_recv()
+    step_rows(1)
     score(0, 0, 0)
     lax.fori_loop(0, SPLIT[0], turn_a, 0)
     sib_copy(7).wait_recv()
@@ -385,8 +389,6 @@
     for c in a_y + b_z:
         c.start()
 
-    lax.fori_loop(SPLIT[0], SPLIT[1], pair, 0)
-
     low, high = pl.ds(0, 2), pl.ds(2, 2)
     a_z = [copy_a(3 + k, fa.at[0], fa.at[d % 8], z_at(d % 8)) for k, d in ((1, 1), (2, -1), (3, 2), (4, -2))]
     a_far = [
@@ -397,18 +399,19 @@
     ]
     b_y = [copy_b(7 + k, fb.at[:, 0], fb.at[:, k], y_at(k)) for k in (1, 3, 2)]
 
+    lax.fori_loop(SPLIT[0], SPLIT[1], pair, 0)
     wait_flip(*flip_a)
     for c in a_y:
         c.wait_recv()
     for c in a_z:
         c.start()
+    lax.fori_loop(SPLIT[1], SPLIT[2], pair, 0)
     wait_flip(*flip_b)
     for c in b_z:
         c.wait_recv()
     for c in b_y:
         c.start()
-
-    lax.fori_loop(SPLIT[1], SPLIT[2], pair, 0)
+    lax.fori_loop(SPLIT[2], SPLIT[3], pair, 0)
 
     def finish(t, carry):
         at = pl.multiple_of(t * HD, HD)
@@ -420,8 +423,7 @@
         c.wait_recv()
     for c in a_far:
         c.start()
-    lax.fori_loop(0, TILES, finish, 0, unroll=2)
-    start_flip(*o_flip)
+    lax.fori_loop(SPLIT[3], SPLIT[4], pair, 0)
 
     r = lax.broadcasted_iota(jnp.int32, (128, 256), 0)
     dz = head * 2 + r // 64
@@ -433,8 +435,8 @@
     wanted = jnp.sum(jnp.where(match, (attr_ref[...] == ctx // 16).astype(F32), 0.0), axis=1, keepdims=True)
 
     w32 = w_out_ref[...].astype(F32)
-    odd = lax.broadcasted_iota(jnp.int32, (256, 128), 1) % 2 == 1
-    w16 = jnp.where(odd, w32[:, 1:2], w32[:, 0:1]).T[0:16, :].astype(BF16)
+    odd = lax.broadcasted_iota(jnp.int32, (16, 256), 0) % 2 == 1
+    w16 = jnp.where(odd, w32[1:2, :], w32[0:1, :]).astype(BF16)
     get_w.wait()
     for c in b_y + a_far:
         c.wait_recv()
@@ -466,6 +468,7 @@
         sends.append(remote(part16.at[at], got.at[step], h_s.at[step], h_r.at[step], head_dev(step)))
     for c in sends:
         c.start()
+    lax.fori_loop(SPLIT[4], SPLIT[5], pair, 0)
     pre = part[pl.ds(pl.multiple_of(head * 128, 128), 128), :]
     squares = square[head]
     for c in sends:
@@ -481,13 +484,15 @@
     line = lax.broadcasted_iota(jnp.int32, (8, 128), 0)
     tile = jnp.where(line < 2, mapped[:, :128], mapped[:, 128:])
 
-    def all_sum(value, buf, send, recv, me, count, at):
+    def all_sum(value, buf, send, recv, me, count, at, beside=None):
         buf[me] = value
         copies = []
         for step in range(1, count):
             copies.append(remote(buf.at[me], buf.at[me], send.at[step], recv.at[step], at(step)))
         for c in copies:
             c.start()
+        if beside is not None:
+            beside()
         for c in copies:
             c.wait_recv()
         total = buf[0]
@@ -495,10 +500,15 @@
             total = total + buf[i]
         return total, copies
 
-    tile, c1 = all_sum(tile, r1, s1, t1, me8, 8, chip_at)
+    def hand_back():
+        lax.fori_loop(0, TILES, finish, 0, unroll=2)
+        start_flip(*o_flip)
+
+    tile, c1 = all_sum(tile, r1, s1, t1, me8, 8, chip_at, hand_back)
     tile, c2 = all_sum(tile, r2, s2, t2, y, 4, y_at)
     tile, c3 = all_sum(tile, r3, s3, t3, z, 8, z_at)
-    logit_ref[...] = tile
+    logit_ref[:, 0:128] = tile[0:2, :]
+    logit_ref[:, 128:256] = tile[2:4, :]
 
     for c in c1 + c2 + c3 + a_y + a_z + a_far + b_z + b_y:
         c.wait_send()
@@ -522,11 +532,11 @@
     vmem = pltpu.VMEM
     here = pl.BlockSpec(memory_space=pltpu.VMEM)
     away = pl.BlockSpec(memory_space=pl.ANY)
-    attended, tile = pl.pallas_call(
+    attended, logits = pl.pallas_call(
         fused_kernel,
         out_shape=(
             jax.ShapeDtypeStruct(queries.shape, BF16),
-            jax.ShapeDtypeStruct((8, 128), F32),
+            jax.ShapeDtypeStruct((2, 256), F32),
         ),
         in_specs=[away] * 4 + [here] * 3,
         out_specs=(here, here),
@@ -571,8 +581,8 @@
             collective_id=0, has_side_effects=True, vmem_limit_bytes=60 * 2**20
         ),
         name="trace_scores",
-    )(queries, keys, values, w_in, w_out, step_pos.reshape(1, 256), step_attr.reshape(1, 256))
-    return attended, jnp.concatenate([tile[0:2], tile[2:4]], axis=1).T
+    )(queries, keys, values, w_in, w_out.T, step_pos.reshape(1, 256), step_attr.reshape(1, 256))
+    return attended, logits.T
 
 
 def solution(mesh):

time: 113 us -> 101 us (0.89)
  Pallas kernels: 105 us -> 95.9 us
  local copies, waits for them, and re-layouts: 4.06 us -> 2.45 us
    pallas_call x1, Pallas kernels: 105 us -> 95.9 us  [body(): pl.pallas_call(fused_kernel, out_shape=(jax.ShapeDtypeStruct(queries.shap...]
    unnamed x2 -> x4, local copies, waits for them, and re-layouts: 3.3 us -> 2.45 us
where the time goes in v3:
time: 101 us; the launch traced here: 99 us
  Pallas kernels  95.9 us (95%)
  local copies, waits for them, and re-layouts  2.45 us (2%)
    pallas_call x1, Pallas kernels, body(): pl.pallas_call(fused_kernel, out_shape=(jax.ShapeDtypeStruct(queries.shap...  95.9 us
    unnamed x4, local copies, waits for them, and re-layouts  2.45 us

profile of v3, /device:TPU:6, one launch (start us, length us, event | category | flops | bytes accessed | tf_op | source)
XLA Modules:
  0.0 99.0 jit_solution(7674689640401745433)
XLA Ops:
  0.6 95.9 %trace_scores.1 = (bf16[256,1024]{1,0:T(8,128)(2,1)}, f32[2,256]{1,0:T(2,128)}) custom-call(bf16[256,1024]{1,0:T(8,128)(2,1)} %q_ref.1, bf16[256,128]{1,0:T(8,128)(2,1)} %k_ref.1, bf16[256,128]{1,0:T(8,128)(2,1)} %v_ref.1, bf16[1024,256]{1,0:T(8,128)(2,1)} %w_ref.1, bf16[2,256]{1,0:T(2,128)(2,1)} %bitcast.5, s32[1,256]{1,0:T(1,128)} %bitcast.6, s32[1,256]{1,0:T(1,128)} %bitcast.7), custom_call_target="tpu_custom_call" | custom-call | tf_op jit(solution)/shard_map/trace_scores/pallas_call | solution.py:535
  96.5 0.0 copy-start
  96.5 1.9 %copy.11 = bf16[256,1024]{1,0:T(8,128)(2,1)} copy(bf16[256,1024]{1,0:T(8,128)(2,1)} %get-tuple-element.8) | data formatting | bytes 1048576
  98.4 0.0 copy-done
  98.4 0.6 copy.12
Async XLA Ops:
  96.5 1.9 %copy-start = (f32[2,256]{1,0:T(2,128)S(1)}, f32[2,256]{1,0:T(2,128)}, u32[]{:S(2)}) copy-start(f32[2,256]{1,0:T(2,128)} %get-tuple-element.5) | copy-start | bytes 6148

commit v4 on v3

--- a/solution.py
+++ b/solution.py
@@ -90,12 +90,20 @@
         pl.semaphore_signal(barrier, inc=1, device_id=target, device_id_type=MESH)
 
     for step in range(1, 8):
-        greet(z_at(step))
-        greet(flip_at(step, 0))
         greet(chip_at(step))
-    for step in range(1, 4):
-        greet(y_at(step))
-        greet(flip_at(0, step))
+    for step in (1, -1):
+        greet(z_dev[step])
+        greet(y_dev[step])
+
+    def greet_far():
+        for step in range(1, 8):
+            if step not in (1, 7):
+                greet(z_at(step))
+            greet(flip_at(step, 0))
+        for step in range(1, 4):
+            if step == 2:
+                greet(y_at(step))
+            greet(flip_at(0, step))
 
     get_k = pltpu.make_async_copy(k_ref, stage.at[pl.ds(0, 256)], load.at[0])
     get_v = pltpu.make_async_copy(v_ref, v_in, load.at[1])
@@ -118,7 +126,7 @@
     stage[384:512, :] = v32[128:256, :].T.astype(BF16)
     get_k.wait()
 
-    pl.semaphore_wait(barrier, 27)
+    pl.semaphore_wait(barrier, 11)
 
     def spot_ref(dz, dy):
         n, j = PLACE[(dz, dy)]
@@ -338,6 +346,8 @@
             @pl.when(step == EVENT[m])
             def _():
                 gather_chunk(m)
+                if m == 6:
+                    greet_far()
 
         due = jnp.int32(1)
         fresh = step == EVENT[2] + 1
@@ -384,6 +394,7 @@
     flip_a = (own_a, fa.at[0, 0], a_s.at[0], a_r.at[0])
     b_z = [copy_b(k, own_b, fb.at[k, 0], flip_at(k, 0)) for k in range(1, 8)]
     a_y = [copy_a(k, own_a, fa.at[0, k], flip_at(0, k)) for k in range(1, 4)]
+    pl.semaphore_wait(barrier, 16)
     start_flip(*flip_a)
     start_flip(*flip_b)
     for c in a_y + b_z:

time: 101 us -> 98.6 us (0.976)
  Pallas kernels: 95.9 us -> 93.8 us
    pallas_call x1, Pallas kernels: 95.9 us -> 93.8 us  [body(): pl.pallas_call(fused_kernel, out_shape=(jax.ShapeDtypeStruct(queries.shap...]
where the time goes in v4:
time: 98.6 us; the launch traced here: 96.9 us
  Pallas kernels  93.8 us (95%)
  local copies, waits for them, and re-layouts  2.45 us (2%)
    pallas_call x1, Pallas kernels, body(): pl.pallas_call(fused_kernel, out_shape=(jax.ShapeDtypeStruct(queries.shap...  93.8 us
    unnamed x4, local copies, waits for them, and re-layouts  2.45 us

profile of v4, /device:TPU:6, one launch (start us, length us, event | category | flops | bytes accessed | tf_op | source)
XLA Modules:
  0.0 96.9 jit_solution(4774663156105218680)
XLA Ops:
  0.6 93.8 %trace_scores.1 = (bf16[256,1024]{1,0:T(8,128)(2,1)}, f32[2,256]{1,0:T(2,128)}) custom-call(bf16[256,1024]{1,0:T(8,128)(2,1)} %q_ref.1, bf16[256,128]{1,0:T(8,128)(2,1)} %k_ref.1, bf16[256,128]{1,0:T(8,128)(2,1)} %v_ref.1, bf16[1024,256]{1,0:T(8,128)(2,1)} %w_ref.1, bf16[2,256]{1,0:T(2,128)(2,1)} %bitcast.5, s32[1,256]{1,0:T(1,128)} %bitcast.6, s32[1,256]{1,0:T(1,128)} %bitcast.7), custom_call_target="tpu_custom_call" | custom-call | tf_op jit(solution)/shard_map/trace_scores/pallas_call | solution.py:546
  94.5 0.0 copy-start
  94.5 1.9 %copy.11 = bf16[256,1024]{1,0:T(8,128)(2,1)} copy(bf16[256,1024]{1,0:T(8,128)(2,1)} %get-tuple-element.8) | data formatting | bytes 1048576
  96.4 0.0 copy-done
  96.4 0.6 copy.12
Async XLA Ops:
  94.5 1.9 %copy-start = (f32[2,256]{1,0:T(2,128)S(1)}, f32[2,256]{1,0:T(2,128)}, u32[]{:S(2)}) copy-start(f32[2,256]{1,0:T(2,128)} %get-tuple-element.5) | copy-start | bytes 6148

commit v5 on v4

--- a/solution.py
+++ b/solution.py
@@ -48,7 +48,7 @@
 
 
 EVENT = (0, 0, 0, 3, 5, 8, 10, 13)
-SPLIT = (14, 18, 21, 24, 29, 32)
+SPLIT = (14, 17, 20, 23, 28, 32)
 
 
 def fused_kernel(
@@ -321,15 +321,24 @@
         update = mix(n, lambda at: scores[slot, at * 256:(at + 1) * 256, :], new[:1])
         acc[t] = acc[t] * fade + update
 
+    def in_sight(n):
+        seen = n < 0
+        for m, chunk in enumerate(CHUNKS):
+            for dz in sorted({spot[0] for spot in chunk}):
+                seen = seen | ((n == m) & ((z + 8 - dz) % 8 <= z))
+        return seen
+
     def step_rows(n):
-        s = jnp.dot(keys_of(n), qs_t[...], preferred_element_type=F32)
-        s_scores[...] = s
-        old = s_top[...]
-        new = jnp.maximum(old, jnp.max(best_of(s, n), axis=0, keepdims=True) * SCALE)
-        s_top[...] = new
-        fade = jnp.exp2(old - new)[:1]
-        update = mix(n, lambda at: s_scores[at * 256:(at + 1) * 256, :], new[:1])
-        s_acc[...] = s_acc[...] * fade + update
+        @pl.when(in_sight(jnp.int32(n)))
+        def _():
+            s = jnp.dot(keys_of(n), qs_t[...], preferred_element_type=F32)
+            s_scores[...] = s
+            old = s_top[...]
+            new = jnp.maximum(old, jnp.max(best_of(s, n), axis=0, keepdims=True) * SCALE)
+            s_top[...] = new
+            fade = jnp.exp2(old - new)[:1]
+            update = mix(n, lambda at: s_scores[at * 256:(at + 1) * 256, :], new[:1])
+            s_acc[...] = s_acc[...] * fade + update
 
     def pair(step, carry):
         n = step // 4

time: 98.6 us -> 98.1 us (level); the launches traced: 96.9 us -> 98 us
  Pallas kernels: 93.8 us -> 94.9 us
    pallas_call x1, Pallas kernels: 93.8 us -> 94.9 us  [body(): pl.pallas_call(fused_kernel, out_shape=(jax.ShapeDtypeStruct(queries.shap...]
where the time goes in v5:
time: 98.1 us; the launch traced here: 98 us
  Pallas kernels  94.9 us (97%)
  local copies, waits for them, and re-layouts  2.45 us (2%)
    pallas_call x1, Pallas kernels, body(): pl.pallas_call(fused_kernel, out_shape=(jax.ShapeDtypeStruct(queries.shap...  94.9 us
    unnamed x4, local copies, waits for them, and re-layouts  2.45 us

profile of v5, /device:TPU:6, one launch (start us, length us, event | category | flops | bytes accessed | tf_op | source)
XLA Modules:
  0.0 98.0 jit_solution(15006746628514544431)
XLA Ops:
  0.6 94.9 %trace_scores.1 = (bf16[256,1024]{1,0:T(8,128)(2,1)}, f32[2,256]{1,0:T(2,128)}) custom-call(bf16[256,1024]{1,0:T(8,128)(2,1)} %q_ref.1, bf16[256,128]{1,0:T(8,128)(2,1)} %k_ref.1, bf16[256,128]{1,0:T(8,128)(2,1)} %v_ref.1, bf16[1024,256]{1,0:T(8,128)(2,1)} %w_ref.1, bf16[2,256]{1,0:T(2,128)(2,1)} %bitcast.5, s32[1,256]{1,0:T(1,128)} %bitcast.6, s32[1,256]{1,0:T(1,128)} %bitcast.7), custom_call_target="tpu_custom_call" | custom-call | tf_op jit(solution)/shard_map/trace_scores/pallas_call | solution.py:555
  95.5 0.0 copy-start
  95.6 1.9 %copy.11 = bf16[256,1024]{1,0:T(8,128)(2,1)} copy(bf16[256,1024]{1,0:T(8,128)(2,1)} %get-tuple-element.8) | data formatting | bytes 1048576
  97.4 0.0 copy-done
  97.4 0.6 copy.12
Async XLA Ops:
  95.5 1.9 %copy-start = (f32[2,256]{1,0:T(2,128)S(1)}, f32[2,256]{1,0:T(2,128)}, u32[]{:S(2)}) copy-start(f32[2,256]{1,0:T(2,128)} %get-tuple-element.5) | copy-start | bytes 6148
